TPU v7x, 1024 devices: a whole 8x8x8 slice. The times are simulated.
1024 devices in a mesh: row: 32 (over x, z_hi, core), col: 32 (over y, z_lo).
Axes of the slice: x: 8, y: 8, z: 8 (z_hi: 2, z_lo: 4; z = z_hi * 4 + z_lo), core: 2. Of those that a mesh axis runs over, the one named last changes fastest.
Arguments:
- a_blocks: bfloat16 [32, 32, 8, 256, 256], P('row', 'col'), may hold values from -0.375 to 0.375
- a_rows: int32 [32, 32, 2, 4], P('row', 'col'), may hold values from -1 to 1, as said below
- b_blocks: bfloat16 [32, 32, 8, 256, 256], P('row', 'col'), may hold values from -6 to 6
- b_cols: int32 [32, 32, 2, 4], P('row', 'col'), may hold values from -1 to 1, as said below
- c_pattern: int32 [32, 32, 3], P('row', 'col'), may hold values from 0 to 3, as said below
Outputs:
- c_blocks: bfloat16 [32, 32, 3, 256, 256], P('row', 'col')
Inputs may be any that keep to these rules, and one draw needn't show every extreme that they name: `a_rows`: each panel has exactly 6 slots that are not -1. `b_cols`: each panel has exactly 6 slots that are not -1. `c_pattern`: the entries of one panel's pattern are distinct.
All inputs are finite; a program needn't handle non-finite values.
Results may differ from a plain program's by a relative error of at most 0.001.
Values may be sent and summed in bfloat16 or wider, within the bound.
A program may use at most 64 MiB of HBM per device.

v0:
```python
import jax
import jax.numpy as jnp
from jax import lax
from jax.sharding import PartitionSpec as P


def from_behind(value, axis, steps):
    count = lax.axis_size(axis)
    pairs = [(source, (source + steps) % count) for source in range(count)]
    return lax.ppermute(value, axis, pairs)


def panel_terms(a_vals, rows, b_vals, cols, pattern):
    panel_rows = rows.shape[0]
    width = rows.shape[1]
    size = a_vals.shape[-1]
    left = a_vals.reshape(panel_rows, width, size, size)
    right = b_vals.reshape(panel_rows, width, size, size)
    products = jnp.einsum("kmxy,knyz->kmnxz", left, right, preferred_element_type=jnp.float32)
    target = rows[:, :, None] * panel_rows + cols[:, None, :]
    valid = (rows[:, :, None] >= 0) & (cols[:, None, :] >= 0)
    target = jnp.where(valid, target, -1).reshape(-1)
    select = (pattern[:, None] == target[None, :]).astype(jnp.float32)
    flat = products.reshape(-1, size, size)
    return jnp.einsum("cq,qxz->cxz", select, flat, precision=lax.Precision.HIGHEST)


def body(a_blocks, a_rows, b_blocks, b_cols, c_pattern):
    size = a_blocks.shape[-1]
    slot_count = a_blocks.shape[2]
    a_vals = a_blocks.reshape(slot_count, size, size)
    b_vals = b_blocks.reshape(slot_count, size, size)
    rows = a_rows.reshape(a_rows.shape[2], a_rows.shape[3])
    cols = b_cols.reshape(b_cols.shape[2], b_cols.shape[3])
    pattern = c_pattern.reshape(-1)
    a_moved, rows_moved = from_behind((a_vals, rows), "row", -1)
    b_moved, cols_moved = from_behind((b_vals, cols), "col", -1)
    first = panel_terms(a_vals, rows, b_vals, cols, pattern)
    second = panel_terms(a_moved, rows_moved, b_moved, cols_moved, pattern)
    total = (first + second).astype(jnp.bfloat16)
    return total.reshape(1, 1, pattern.shape[0], size, size)


def solution(mesh):
    in_specs = (
        P("row", "col", None, None, None),
        P("row", "col", None, None),
        P("row", "col", None, None, None),
        P("row", "col", None, None),
        P("row", "col", None),
    )
    out_specs = P("row", "col", None, None, None)
    return jax.shard_map(body, mesh=mesh, in_specs=in_specs, out_specs=out_specs, check_vma=False)
```

profile of v0, /device:TPU:55, one launch (start us, length us, event | category | flops | bytes accessed | tf_op | source)
XLA Modules:
  0.0 102.7 jit_solution(17613166941481469128)
XLA Ops:
  0.0 10.1 %collective-permute-start.2 = (bf16[8,256,256]{2,1,0:T(8,128)(2,1)}, bf16[8,256,256]{2,1,0:T(8,128)(2,1)S(1)}, u32[]{:S(2)}, u32[]{:S(2)}) collective-permute-start(bf16[8,256,256]{2,1,0:T(8,128)(2,1)} %bitcast.49), channel_id=1, source_target_pairs={{0,31},{1,0},{2,1},{3,2},{4,3},{5,4},{6,5},{7,6},{8,7},{9,8},{10,9... | collective-permute-start | bytes 3145736 | tf_op jit(solution)/shard_map/ppermute | solution.py:10
  10.1 2.9 %collective-permute-start.3 = (bf16[8,256,256]{2,1,0:T(8,128)(2,1)}, bf16[8,256,256]{2,1,0:T(8,128)(2,1)S(1)}, u32[]{:S(2)}, u32[]{:S(2)}) collective-permute-start(bf16[8,256,256]{2,1,0:T(8,128)(2,1)} %bitcast.51), channel_id=1, source_target_pairs={{0,992},{32,0},{64,32},{96,64},{128,96},{160,128},{192,160},{224,1... | collective-permute-start | bytes 3145736 | tf_op jit(solution)/shard_map/ppermute | solution.py:10
  13.0 1.9 %collective-permute-start.1 = (s32[2,4]{1,0:T(2,128)}, s32[2,4]{1,0:T(2,128)S(1)}, u32[]{:S(2)}, u32[]{:S(2)}) collective-permute-start(s32[2,4]{1,0:T(2,128)} %bitcast.57), channel_id=1, source_target_pairs={{0,31},{1,0},{2,1},{3,2},{4,3},{5,4},{6,5},{7,6},{8,7},{9,8},{10,9... | collective-permute-start | bytes 104 | tf_op jit(solution)/shard_map/ppermute | solution.py:10
  14.9 11.3 %collective-permute-start = (s32[2,4]{1,0:T(2,128)}, s32[2,4]{1,0:T(2,128)S(1)}, u32[]{:S(2)}, u32[]{:S(2)}) collective-permute-start(s32[2,4]{1,0:T(2,128)} %bitcast.59), channel_id=1, source_target_pairs={{0,992},{32,0},{64,32},{96,64},{128,96},{160,128},{192,160},{224,1... | collective-permute-start | bytes 104 | tf_op jit(solution)/shard_map/ppermute | solution.py:10
  26.2 0.7 broadcast_multiply_fusion.1
  26.9 0.7 broadcast_compare_fusion.2
  27.6 0.7 broadcast_compare_fusion.3
  28.2 6.3 %convolution_bitcast_fusion.1 = f32[2,4,4,256,256]{3,4,1,2,0:T(8,128)} fusion(bf16[2,4,256,256,1]{3,2,4,1,0:T(8,128)(2,1)} %bitcast.50, bf16[2,4,256,256,1]{3,2,1,4,0:T(8,128)(2,1)} %bitcast.52), kind=kOutput, calls=%fused_computation.5 | convolution fusion | flops 1073741824 | bytes 10485760 | tf_op jit(solution)/shard_map/kmxy,knyz->kmnxz/dot_general | solution.py:19
  34.5 0.0 copy-start.2
  34.5 9.9 %copy.10 = f32[2,4,4,256,256]{4,3,2,1,0:T(8,128)} copy(f32[2,4,4,256,256]{3,4,1,2,0:T(8,128)} %convolution_bitcast_fusion.1) | data formatting | bytes 16777216 | tf_op jit(solution)/shard_map/kmxy,knyz->kmnxz/transpose | solution.py:19
  44.5 0.0 copy-done.2
  44.5 0.1 add_select_fusion.1
  44.6 0.1 select_n.22
  44.6 14.2 %collective-permute-done.1 = s32[2,4]{1,0:T(2,128)S(1)} collective-permute-done((s32[2,4]{1,0:T(2,128)}, s32[2,4]{1,0:T(2,128)S(1)}, u32[]{:S(2)}, u32[]{:S(2)}) %collective-permute-start.1) | collective-permute-done | bytes 64 | tf_op jit(solution)/shard_map/ppermute | solution.py:10
  58.8 9.5 %collective-permute-done = s32[2,4]{1,0:T(2,128)S(1)} collective-permute-done((s32[2,4]{1,0:T(2,128)}, s32[2,4]{1,0:T(2,128)S(1)}, u32[]{:S(2)}, u32[]{:S(2)}) %collective-permute-start) | collective-permute-done | bytes 64 | tf_op jit(solution)/shard_map/ppermute | solution.py:10
  68.3 0.1 add_select_fusion
  68.4 0.1 select_n.24
  68.5 0.0 collective-permute-done.2
  68.5 0.0 collective-permute-done.3
  68.5 4.7 %convolution_bitcast_fusion = f32[2,4,4,256,256]{3,4,1,2,0:T(8,128)} fusion(bf16[2,4,256,256,1]{3,2,4,1,0:T(8,128)(2,1)S(1)} %bitcast.53, bf16[2,4,256,256,1]{3,2,1,4,0:T(8,128)(2,1)S(1)} %bitcast.54), kind=kOutput, calls=%fused_computation.4 | convolution fusion | flops 1073741824 | bytes 10485760 | tf_op jit(solution)/shard_map/kmxy,knyz->kmnxz/dot_general | solution.py:19
  73.3 0.0 copy-start.1
  73.3 9.9 %copy.13 = f32[2,4,4,256,256]{4,3,2,1,0:T(8,128)} copy(f32[2,4,4,256,256]{3,4,1,2,0:T(8,128)} %convolution_bitcast_fusion) | data formatting | bytes 16777216 | tf_op jit(solution)/shard_map/kmxy,knyz->kmnxz/transpose | solution.py:19
  83.2 0.0 copy-start
  83.2 0.0 copy-done.1
  83.2 10.6 %fusion = f32[3,256,256]{2,0,1:T(4,128)S(1)} fusion(f32[32,256,256]{2,1,0:T(8,128)} %bitcast.48, s32[32]{0:T(128)S(1)} %select_n.24, s32[3]{0:T(128)S(1)} %bitcast.55), kind=kOutput, calls=%fused_computation | convolution fusion | flops 75497568 | bytes 9175180 | tf_op jit(solution)/shard_map/cq,qxz->cxz/dot_general | solution.py:25
  93.8 0.0 copy-done
  93.8 8.1 %fusion.10 = bf16[1,1,3,256,256]{4,2,3,1,0:T(4,128)(2,1)S(1)} fusion(f32[3,256,256]{2,0,1:T(4,128)S(1)} %fusion, f32[32,256,256]{2,1,0:T(8,128)S(1)} %bitcast.47, s32[32]{0:T(128)S(1)} %select_n.22, s32[3]{0:T(128)S(1)} %bitcast.56), kind=kOutput, calls=%fused_computation.8 | convolution fusion | flops 75890784 | bytes 9568396 | tf_op jit(solution)/shard_map/cq,qxz->cxz/dot_general | solution.py:25
  101.9 0.8 copy.15
  (3 shorter events, 0.0 us)
Async XLA Ops:
  0.0 68.5 %collective-permute-start.2 = (bf16[8,256,256]{2,1,0:T(8,128)(2,1)}, bf16[8,256,256]{2,1,0:T(8,128)(2,1)S(1)}, u32[]{:S(2)}, u32[]{:S(2)}) collective-permute-start(bf16[8,256,256]{2,1,0:T(8,128)(2,1)} %bitcast.49), channel_id=1, source_target_pairs={{0,31},{1,0},{2,1},{3,2},{4,3},{5,4},{6,5},{7,6},{8,7},{9,8},{10,9... | collective-permute-start | bytes 3145736 | tf_op jit(solution)/shard_map/ppermute | solution.py:10
  10.1 58.4 %collective-permute-start.3 = (bf16[8,256,256]{2,1,0:T(8,128)(2,1)}, bf16[8,256,256]{2,1,0:T(8,128)(2,1)S(1)}, u32[]{:S(2)}, u32[]{:S(2)}) collective-permute-start(bf16[8,256,256]{2,1,0:T(8,128)(2,1)} %bitcast.51), channel_id=1, source_target_pairs={{0,992},{32,0},{64,32},{96,64},{128,96},{160,128},{192,160},{224,1... | collective-permute-start | bytes 3145736 | tf_op jit(solution)/shard_map/ppermute | solution.py:10
  13.0 45.8 %collective-permute-start.1 = (s32[2,4]{1,0:T(2,128)}, s32[2,4]{1,0:T(2,128)S(1)}, u32[]{:S(2)}, u32[]{:S(2)}) collective-permute-start(s32[2,4]{1,0:T(2,128)} %bitcast.57), channel_id=1, source_target_pairs={{0,31},{1,0},{2,1},{3,2},{4,3},{5,4},{6,5},{7,6},{8,7},{9,8},{10,9... | collective-permute-start | bytes 104 | tf_op jit(solution)/shard_map/ppermute | solution.py:10
  14.9 53.4 %collective-permute-start = (s32[2,4]{1,0:T(2,128)}, s32[2,4]{1,0:T(2,128)S(1)}, u32[]{:S(2)}, u32[]{:S(2)}) collective-permute-start(s32[2,4]{1,0:T(2,128)} %bitcast.59), channel_id=1, source_target_pairs={{0,992},{32,0},{64,32},{96,64},{128,96},{160,128},{192,160},{224,1... | collective-permute-start | bytes 104 | tf_op jit(solution)/shard_map/ppermute | solution.py:10
  34.5 9.9 %copy-start.2 = (s32[1,1,2,4]{3,2,1,0:T(2,128)S(1)}, s32[1,1,2,4]{3,2,1,0:T(2,128)}, u32[]{:S(2)}) copy-start(s32[1,1,2,4]{3,2,1,0:T(2,128)} %param.8) | copy-start | bytes 100
  73.3 9.9 %copy-start.1 = (s32[1,1,3]{2,1,0:T(1,128)S(1)}, s32[1,1,3]{2,1,0:T(1,128)}, u32[]{:S(2)}) copy-start(s32[1,1,3]{2,1,0:T(1,128)} %param.9) | copy-start | bytes 40
  83.2 10.6 %copy-start = (f32[2,4,4,256,256]{4,3,2,1,0:T(8,128)S(1)}, f32[2,4,4,256,256]{4,3,2,1,0:T(8,128)}, u32[]{:S(2)}) copy-start(f32[2,4,4,256,256]{4,3,2,1,0:T(8,128)} %copy.10) | copy-start | bytes 25165828
where the time goes:
time: 103 us
  matrix products  29.7 us (29%)
  starting transfers between devices  26.2 us (25%)
  waiting for transfers between devices  23.7 us (23%)
  local copies, waits for them, and re-layouts  20.9 us (20%)
  other arithmetic  2.21 us (2%)
    ppermute x4, starting transfers between devices, from_behind(): return lax.ppermute(value, axis, pairs)  26.2 us
    ppermute x4, waiting for transfers between devices, from_behind(): return lax.ppermute(value, axis, pairs)  23.7 us
    transpose x2, local copies, waits for them, and re-layouts, panel_terms(): jnp.einsum('kmxy,knyz->kmnxz', left, right, preferred_element_type=jnp.fl...  19.9 us
    dot_general x2, matrix products, panel_terms(): jnp.einsum('cq,qxz->cxz', select, flat, precision=lax.Precision.HIGHEST)  18.7 us
    dot_general x2, matrix products, panel_terms(): jnp.einsum('kmxy,knyz->kmnxz', left, right, preferred_element_type=jnp.fl...  11 us
  transfers between devices with their start and end apart: 4, of which 2 were waited for; matrix products, arithmetic and copies ran while one was open for 18% of the time, Pallas kernels for 0%

commit v1 on v0

v1 whole, which is shorter than its diff:
```python
import jax
import jax.numpy as jnp
from jax import lax
from jax.experimental import pallas as pl
from jax.experimental.pallas import tpu as pltpu
from jax.sharding import PartitionSpec as P

MESH = pl.DeviceIdType.MESH
TINY = 1.2e-34
TOP = 32767.0


def split(value):
    high = value.astype(jnp.bfloat16)
    low = (value - high.astype(jnp.float32)).astype(jnp.bfloat16)
    return high, low


def kernel(
    a_hbm, rows, b_hbm, cols, pattern, out,
    a_in, b_in, a_send, b_send, a_got, b_got, a_scale, b_scale, a_scale_got, b_scale_got,
    a_high, a_low, b_high, b_low, total,
    load_sem, a_send_sem, a_recv_sem, b_send_sem, b_recv_sem,
):
    n_row, n_col = lax.axis_size("row"), lax.axis_size("col")
    r, c = lax.axis_index("row"), lax.axis_index("col")
    panel_rows, width = rows.shape[2], rows.shape[3]
    size = a_in.shape[-1]

    loads = []
    for k in range(panel_rows):
        part = pl.ds(k * width, width)
        for n, (source, target) in enumerate(((a_hbm, a_in), (b_hbm, b_in))):
            copy = pltpu.make_async_copy(source.at[0, 0, part], target.at[part], load_sem.at[n, k])
            copy.start()
            loads.append(copy)

    barrier = pltpu.get_barrier_semaphore()
    below = lax.rem(r + n_row - 1, n_row)
    left = lax.rem(c + n_col - 1, n_col)
    pl.semaphore_signal(barrier, inc=1, device_id=(lax.rem(r + 1, n_row), c), device_id_type=MESH)
    pl.semaphore_signal(barrier, inc=1, device_id=(r, lax.rem(c + 1, n_col)), device_id_type=MESH)

    def send(source, target, sems, at, device):
        return pltpu.make_async_remote_copy(
            src_ref=source, dst_ref=target, send_sem=sems[0].at[at], recv_sem=sems[1].at[at],
            device_id=device, device_id_type=MESH,
        )

    def coded(value, queue, scale, at):
        peak = jnp.maximum(jnp.max(jnp.abs(value), axis=0, keepdims=True), TINY)
        queue[at] = jnp.round(value * (TOP / peak)).astype(jnp.int32).astype(jnp.int16)
        scale[pl.ds(at, 1), :] = peak * (1.0 / TOP)

    def summed(labels, blocks, k, want):
        value = None
        for m in range(width):
            weight = (labels[0, 0, k, m] == want).astype(jnp.float32)
            term = blocks[k * width + m].astype(jnp.float32) * weight
            value = term if value is None else value + term
        return value

    copies = []
    a_sems, b_sems = (a_send_sem, a_recv_sem), (b_send_sem, b_recv_sem)
    a_to, b_to = (below, c), (r, left)
    for k in range(panel_rows):
        span = pl.ds(k * size, size)
        loads[2 * k].wait()
        for i in range(panel_rows):
            at = k * panel_rows + i
            value = summed(rows, a_in, k, i)
            coded(value, a_send, a_scale, at)
            a_high[i, :, span], a_low[i, :, span] = split(value)
            if k == 0 and i == 0:
                pl.semaphore_wait(barrier, 2)
            copy = send(a_send.at[at], a_got.at[at], a_sems, at, a_to)
            copy.start()
            copies.append(copy)
        loads[2 * k + 1].wait()
        for j in range(panel_rows):
            at = k * panel_rows + j
            value = summed(cols, b_in, k, j)
            coded(value, b_send, b_scale, at)
            b_high[j, span, :], b_low[j, span, :] = split(value)
            copy = send(b_send.at[at], b_got.at[at], b_sems, at, b_to)
            copy.start()
            copies.append(copy)
    last = panel_rows * panel_rows
    for copy in (
        send(a_scale, a_scale_got, a_sems, last, a_to),
        send(b_scale, b_scale_got, b_sems, last, b_to),
    ):
        copy.start()
        copies.append(copy)

    def product(target):
        i, j = target >> 1, target & 1
        ah, al, bh, bl = a_high[i], a_low[i], b_high[j], b_low[j]
        dot = lambda x, y: jnp.dot(x, y, preferred_element_type=jnp.float32)
        return dot(ah, bh) + (dot(ah, bl) + dot(al, bh) + dot(al, bl))

    kept = pattern.shape[2]
    for n in range(kept):
        total[n] = product(pattern[0, 0, n])

    for copy in copies:
        copy.wait_send()
    for copy in copies:
        copy.wait_recv()
    for k in range(panel_rows):
        span = pl.ds(k * size, size)
        for i in range(panel_rows):
            at = k * panel_rows + i
            value = a_got[at].astype(jnp.int32).astype(jnp.float32) * a_scale_got[pl.ds(at, 1), :]
            a_high[i, :, span], a_low[i, :, span] = split(value)
            value = b_got[at].astype(jnp.int32).astype(jnp.float32) * b_scale_got[pl.ds(at, 1), :]
            b_high[i, span, :], b_low[i, span, :] = split(value)
    for n in range(kept):
        out[0, 0, n] = (total[n] + product(pattern[0, 0, n])).astype(out.dtype)


def body(a_blocks, a_rows, b_blocks, b_cols, c_pattern):
    slots, size = a_blocks.shape[2], a_blocks.shape[-1]
    panel_rows = a_rows.shape[2]
    kept = c_pattern.shape[2]
    groups = panel_rows * panel_rows
    smem = pl.BlockSpec(memory_space=pltpu.SMEM)
    anywhere = pl.BlockSpec(memory_space=pl.ANY)
    bf16, f32 = jnp.bfloat16, jnp.float32
    depth = panel_rows * size
    queue = pltpu.VMEM((groups, size, size), jnp.int16)
    scale = pltpu.VMEM((8, size), f32)
    sems = pltpu.SemaphoreType.DMA((groups + 1,))
    return pl.pallas_call(
        kernel,
        out_shape=jax.ShapeDtypeStruct((1, 1, kept, size, size), bf16),
        in_specs=[anywhere, smem, anywhere, smem, smem],
        out_specs=pl.BlockSpec(memory_space=pltpu.VMEM),
        scratch_shapes=[
            pltpu.VMEM((slots, size, size), bf16), pltpu.VMEM((slots, size, size), bf16),
            queue, queue, queue, queue, scale, scale, scale, scale,
            pltpu.VMEM((panel_rows, size, depth), bf16), pltpu.VMEM((panel_rows, size, depth), bf16),
            pltpu.VMEM((panel_rows, depth, size), bf16), pltpu.VMEM((panel_rows, depth, size), bf16),
            pltpu.VMEM((kept, size, size), f32),
            pltpu.SemaphoreType.DMA((2, panel_rows)), sems, sems, sems, sems,
        ],
        compiler_params=pltpu.CompilerParams(
            collective_id=0, has_side_effects=True, vmem_limit_bytes=60 << 20
        ),
        cost_estimate=pl.CostEstimate(flops=64 * 2 * size**3, bytes_accessed=3 << 20, transcendentals=0),
    )(a_blocks, a_rows, b_blocks, b_cols, c_pattern)


def solution(mesh):
    in_specs = (
        P("row", "col", None, None, None),
        P("row", "col", None, None),
        P("row", "col", None, None, None),
        P("row", "col", None, None),
        P("row", "col", None),
    )
    out_specs = P("row", "col", None, None, None)
    return jax.shard_map(body, mesh=mesh, in_specs=in_specs, out_specs=out_specs, check_vma=False)
```

time: 103 us -> 51.2 us (0.50)
  the two profiles are of different devices: /device:TPU:55 before, /device:TPU:127 now
where the time goes in v1:
time: 51.2 us; the launch traced here: 51 us
  Pallas kernels  49.2 us (96%)
  local copies, waits for them, and re-layouts  1.77 us (3%)
    pallas_call x1, Pallas kernels, body(): pl.pallas_call(kernel, out_shape=jax.ShapeDtypeStruct((1, 1, kept, size,...  49.2 us
    unnamed x1, local copies, waits for them, and re-layouts  1.77 us

profile of v1, /device:TPU:127, one launch (start us, length us, event | category | flops | bytes accessed | tf_op | source)
XLA Modules:
  0.0 51.0 jit_solution(17996493801374351420)
XLA Ops:
  0.0 49.2 %shard_map.55 = bf16[1,1,3,256,256]{4,3,2,1,0:T(8,128)(2,1)} custom-call(bf16[1,1,8,256,256]{4,3,2,1,0:T(8,128)(2,1)} %a_hbm.1, s32[1,1,2,4]{3,2,1,0:T(2,128)} %rows.1, bf16[1,1,8,256,256]{4,3,2,1,0:T(8,128)(2,1)} %b_hbm.1, s32[1,1,2,4]{3,2,1,0:T(2,128)} %cols.1, s32[1,1,3]{2,1,0:T(1,128)} %pattern.1), custom_call_target="tpu_custom_call" | custom-call | flops 2147483648 | bytes 3145728 | tf_op jit(solution)/shard_map/pallas_call | solution.py:134
  49.2 1.8 %copy.7 = bf16[1,1,3,256,256]{4,3,2,1,0:T(8,128)(2,1)} copy(bf16[1,1,3,256,256]{4,3,2,1,0:T(8,128)(2,1)} %shard_map.55) | data formatting | bytes 786432

commit v2 on v1

v2 whole, which is shorter than its diff:
```python
import functools

import jax
import jax.numpy as jnp
from jax import lax
from jax.experimental import pallas as pl
from jax.experimental.pallas import tpu as pltpu
from jax.sharding import PartitionSpec as P

MESH = pl.DeviceIdType.MESH
TINY = 1.2e-34
TOP = 32767.0
RETURNED = 0b0
HOLDS = 0b10110000


def split(value):
    high = value.astype(jnp.bfloat16)
    low = (value - high.astype(jnp.float32)).astype(jnp.bfloat16)
    return high, low


def kernel(
    a_hbm, rows, b_hbm, cols, pattern, out,
    a_in, b_in, a_send, b_send, c_send, a_got, b_got, c_got,
    a_scale, b_scale, c_scale, a_scale_got, b_scale_got, c_scale_got,
    a_high, a_low, b_high, b_low, far_a_high, far_a_low, far_b_high, far_b_low, total,
    load_sem, a_send_sem, b_send_sem, c_send_sem, a_recv_sem, b_recv_sem, c_recv_sem, below_in, left_in, sent,
):
    n_row, n_col = lax.axis_size("row"), lax.axis_size("col")
    r, c = lax.axis_index("row"), lax.axis_index("col")
    panel_rows, width = rows.shape[2], rows.shape[3]
    size = a_in.shape[-1]
    groups = panel_rows * panel_rows
    both, either, no = jnp.logical_and, jnp.logical_or, jnp.logical_not

    core, half, lane = lax.rem(r, 2), lax.rem(lax.div(r, 2), 2), lax.rem(c, 4)
    late = half == 1
    early = no(late)

    def listed(table, half, lane):
        return lax.rem(lax.shift_right_logical(table, half * 4 + lane), 2)

    near, far = core == 1, core == 0
    shift = jnp.where(far, listed(RETURNED, 1 - half, lane), 0)
    is_returned = both(near, listed(RETURNED, half, lane) == 1)
    serves = both(near, listed(RETURNED, half, lax.rem(lane + 3, 4)) == 1)
    holds_b = both(late, listed(HOLDS, half, lane) == 1)
    holds_a = both(early, listed(HOLDS, half, lane) == 1)
    takes_a, sends_b = no(is_returned), no(serves)

    c_up, c_left = lax.rem(c + 1, n_col), lax.rem(c + n_col - 1, n_col)
    r_up = lax.rem(r + 1, n_row)
    target = (lax.rem(r + n_row - 1, n_row), lax.rem(c + shift, n_col))
    up, across = (r_up, c), (r_up, c_left)
    right, left = (r, c_up), (r, c_left)

    loads = []
    for k in range(panel_rows):
        part = pl.ds(k * width, width)
        for n, (source, into) in enumerate(((a_hbm, a_in), (b_hbm, b_in))):
            copy = pltpu.make_async_copy(source.at[0, 0, part], into.at[part], load_sem.at[n, k])
            copy.start()
            loads.append(copy)

    barrier = pltpu.get_barrier_semaphore()
    target_later = either(near, early)
    source_later = both(near, early)
    right_later, left_later = lane < 3, lane == 0

    def signal(sem, device):
        pl.semaphore_signal(sem, inc=1, device_id=device, device_id_type=MESH)

    before = 0
    for there, later, device in (
        (takes_a, source_later, up),
        (serves, source_later, across),
        (core >= 0, target_later, target),
        (core >= 0, right_later, right),
        (core >= 0, left_later, left),
    ):
        pl.when(both(there, later))(functools.partial(signal, barrier, device))
        before = before + jnp.where(both(there, no(later)), 1, 0)

    @pl.when(before > 0)
    def _():
        pl.semaphore_wait(barrier, before)

    pl.when(both(takes_a, no(source_later)))(functools.partial(signal, below_in, up))
    pl.when(both(serves, no(source_later)))(functools.partial(signal, below_in, across))
    pl.when(no(right_later))(functools.partial(signal, left_in, right))

    def await_target():
        @pl.when(target_later)
        def _():
            pl.semaphore_wait(below_in, 1)

    def await_left():
        @pl.when(left_later)
        def _():
            pl.semaphore_wait(left_in, 1)

    def send(source, into, send_sem, recv_sem, device):
        return pltpu.make_async_remote_copy(
            src_ref=source, dst_ref=into, send_sem=send_sem, recv_sem=recv_sem,
            device_id=device, device_id_type=MESH,
        )

    def a_copy(at, slot):
        sems = a_send_sem.at[at], a_recv_sem.at[slot, at]
        if at == groups:
            return send(a_scale, a_scale_got.at[slot], *sems, target)
        return send(a_send.at[at], a_got.at[slot, at], *sems, target)

    def b_copy(at):
        sems = b_send_sem.at[at], b_recv_sem.at[at]
        if at == groups:
            return send(b_scale, b_scale_got, *sems, left)
        return send(b_send.at[at], b_got.at[at], *sems, left)

    def c_copy(at):
        sems = c_send_sem.at[at], c_recv_sem.at[at]
        if at == groups:
            return send(c_scale, c_scale_got, *sems, left)
        return send(c_send.at[at], c_got.at[at], *sems, left)

    def each(copy, act, *more):
        for at in range(groups + 1):
            getattr(copy(at, *more), act)()

    def coded(value, queue, scale, at):
        peak = jnp.maximum(jnp.max(jnp.abs(value), axis=0, keepdims=True), TINY)
        queue[at] = jnp.round(value * (TOP / peak)).astype(jnp.int32).astype(jnp.int16)
        scale[pl.ds(at, 1), :] = peak * (1.0 / TOP)

    def decoded(queue, scale, at):
        return queue[at].astype(jnp.int32).astype(jnp.float32) * scale[pl.ds(at, 1), :]

    def summed(labels, blocks, k, want):
        value = None
        for m in range(width):
            weight = (labels[0, 0, k, m] == want).astype(jnp.float32)
            term = blocks[k * width + m].astype(jnp.float32) * weight
            value = term if value is None else value + term
        return value

    def prepare_a():
        for k in range(panel_rows):
            span = pl.ds(k * size, size)
            loads[2 * k].wait()
            for i in range(panel_rows):
                at = k * panel_rows + i
                value = summed(rows, a_in, k, i)
                coded(value, a_send, a_scale, at)
                a_high[i, :, span], a_low[i, :, span] = split(value)
                yield at

    def prepare_b():
        for k in range(panel_rows):
            span = pl.ds(k * size, size)
            loads[2 * k + 1].wait()
            for j in range(panel_rows):
                at = k * panel_rows + j
                value = summed(cols, b_in, k, j)
                coded(value, b_send, b_scale, at)
                b_high[j, span, :], b_low[j, span, :] = split(value)
                yield at

    @pl.when(early)
    def _():
        for at in prepare_b():
            if at == 0:
                await_left()
            pl.when(sends_b)(b_copy(at).start)
        pl.when(sends_b)(b_copy(groups).start)
        for at in prepare_a():
            pass

    @pl.when(late)
    def _():
        for at in prepare_a():
            pl.when(far)(a_copy(at, shift).start)
        pl.when(far)(a_copy(groups, shift).start)
        for at in prepare_b():
            pass

    @pl.when(near)
    def _():
        await_target()
        each(a_copy, "start", 0)

    @pl.when(late)
    def _():
        await_left()
        pl.when(both(sends_b, no(holds_b)))(functools.partial(each, b_copy, "start"))

    def product(i, j, ah, al, bh, bl):
        ah, al, bh, bl = ah[i], al[i], bh[j], bl[j]
        dot = lambda x, y: jnp.dot(x, y, preferred_element_type=jnp.float32)
        return dot(ah, bh) + (dot(ah, bl) + dot(al, bh) + dot(al, bl))

    kept = pattern.shape[2]
    for n in range(kept):
        block = pattern[0, 0, n]
        total[n] = product(block >> 1, block & 1, a_high, a_low, b_high, b_low)

    @pl.when(both(early, far))
    def _():
        await_target()
        pl.when(both(sends_b, holds_a))(functools.partial(each, b_copy, "wait_send"))
        each(a_copy, "start", shift)

    @pl.when(holds_b)
    def _():
        @pl.when(far)
        def _():
            each(a_copy, "wait_send", shift)
            signal(sent, up)

        @pl.when(near)
        def _():
            pl.semaphore_wait(sent, 1)

        pl.when(sends_b)(functools.partial(each, b_copy, "start"))

    def take_a(slot, high, low):
        each(a_copy, "wait_recv", slot)
        for k in range(panel_rows):
            span = pl.ds(k * size, size)
            for i in range(panel_rows):
                value = decoded(a_got.at[slot], a_scale_got.at[slot], k * panel_rows + i)
                high[i, :, span], low[i, :, span] = split(value)

    def take_b():
        each(b_copy, "wait_recv")
        for k in range(panel_rows):
            span = pl.ds(k * size, size)
            for j in range(panel_rows):
                value = decoded(b_got, b_scale_got, k * panel_rows + j)
                far_b_high[j, span, :], far_b_low[j, span, :] = split(value)

    def serve():
        take_a(1, far_a_high, far_a_low)
        for i in range(panel_rows):
            for j in range(panel_rows):
                at = i * panel_rows + j
                coded(product(i, j, far_a_high, far_a_low, b_high, b_low), c_send, c_scale, at)
                c_copy(at).start()
        c_copy(groups).start()

    pl.when(both(serves, late))(serve)

    @pl.when(both(takes_a, early))
    def _():
        take_b()
        take_a(0, a_high, a_low)

    @pl.when(both(takes_a, late))
    def _():
        take_a(0, a_high, a_low)
        take_b()

    @pl.when(takes_a)
    def _():
        for n in range(kept):
            block = pattern[0, 0, n]
            value = product(block >> 1, block & 1, a_high, a_low, far_b_high, far_b_low)
            out[0, 0, n] = (total[n] + value).astype(out.dtype)

    pl.when(both(serves, early))(serve)

    @pl.when(is_returned)
    def _():
        each(c_copy, "wait_recv")
        for n in range(kept):
            value = decoded(c_got, c_scale_got, pattern[0, 0, n])
            out[0, 0, n] = (total[n] + value).astype(out.dtype)

    @pl.when(no(both(far, holds_b)))
    def _():
        each(a_copy, "wait_send", shift)

    @pl.when(both(sends_b, no(both(far, holds_a))))
    def _():
        each(b_copy, "wait_send")

    @pl.when(serves)
    def _():
        each(c_copy, "wait_send")


def body(a_blocks, a_rows, b_blocks, b_cols, c_pattern):
    slots, size = a_blocks.shape[2], a_blocks.shape[-1]
    panel_rows = a_rows.shape[2]
    kept = c_pattern.shape[2]
    groups = panel_rows * panel_rows
    smem = pl.BlockSpec(memory_space=pltpu.SMEM)
    anywhere = pl.BlockSpec(memory_space=pl.ANY)
    bf16, f32 = jnp.bfloat16, jnp.float32
    depth = panel_rows * size
    queue = pltpu.VMEM((groups, size, size), jnp.int16)
    scale = pltpu.VMEM((8, size), f32)
    regular = pltpu.SemaphoreType.REGULAR
    sems = pltpu.SemaphoreType.DMA((groups + 1,))
    return pl.pallas_call(
        kernel,
        out_shape=jax.ShapeDtypeStruct((1, 1, kept, size, size), bf16),
        in_specs=[anywhere, smem, anywhere, smem, smem],
        out_specs=pl.BlockSpec(memory_space=pltpu.VMEM),
        scratch_shapes=[
            pltpu.VMEM((slots, size, size), bf16), pltpu.VMEM((slots, size, size), bf16),
            queue, queue, queue, pltpu.VMEM((2, groups, size, size), jnp.int16), queue, queue,
            scale, scale, scale, pltpu.VMEM((2, 8, size), f32), scale, scale,
            pltpu.VMEM((panel_rows, size, depth), bf16), pltpu.VMEM((panel_rows, size, depth), bf16),
            pltpu.VMEM((panel_rows, depth, size), bf16), pltpu.VMEM((panel_rows, depth, size), bf16),
            pltpu.VMEM((panel_rows, size, depth), bf16), pltpu.VMEM((panel_rows, size, depth), bf16),
            pltpu.VMEM((panel_rows, depth, size), bf16), pltpu.VMEM((panel_rows, depth, size), bf16),
            pltpu.VMEM((kept, size, size), f32),
            pltpu.SemaphoreType.DMA((2, panel_rows)), sems, sems, sems,
            pltpu.SemaphoreType.DMA((2, groups + 1)), sems, sems, regular, regular, regular,
        ],
        compiler_params=pltpu.CompilerParams(
            collective_id=0, has_side_effects=True, vmem_limit_bytes=60 << 20
        ),
        cost_estimate=pl.CostEstimate(flops=64 * 2 * size**3, bytes_accessed=3 << 20, transcendentals=0),
    )(a_blocks, a_rows, b_blocks, b_cols, c_pattern)


def solution(mesh):
    in_specs = (
        P("row", "col", None, None, None),
        P("row", "col", None, None),
        P("row", "col", None, None, None),
        P("row", "col", None, None),
        P("row", "col", None),
    )
    out_specs = P("row", "col", None, None, None)
    return jax.shard_map(body, mesh=mesh, in_specs=in_specs, out_specs=out_specs, check_vma=False)
```

time: 51.2 us -> 39.7 us (0.78)
  the two profiles are of different devices: /device:TPU:127 before, /device:TPU:319 now
where the time goes in v2:
time: 39.7 us; the launch traced here: 39.5 us
  Pallas kernels  37.7 us (95%)
  local copies, waits for them, and re-layouts  1.77 us (4%)
    pallas_call x1, Pallas kernels, body(): pl.pallas_call(kernel, out_shape=jax.ShapeDtypeStruct((1, 1, kept, size,...  37.7 us
    unnamed x1, local copies, waits for them, and re-layouts  1.77 us

profile of v2, /device:TPU:319, one launch (start us, length us, event | category | flops | bytes accessed | tf_op | source)
XLA Modules:
  0.0 39.5 jit_solution(634544674376614484)
XLA Ops:
  0.0 37.7 %shard_map.55 = bf16[1,1,3,256,256]{4,3,2,1,0:T(8,128)(2,1)} custom-call(bf16[1,1,8,256,256]{4,3,2,1,0:T(8,128)(2,1)} %a_hbm.1, s32[1,1,2,4]{3,2,1,0:T(2,128)} %rows.1, bf16[1,1,8,256,256]{4,3,2,1,0:T(8,128)(2,1)} %b_hbm.1, s32[1,1,2,4]{3,2,1,0:T(2,128)} %cols.1, s32[1,1,3]{2,1,0:T(1,128)} %pattern.1), custom_call_target="tpu_custom_call" | custom-call | flops 2147483648 | bytes 3145728 | tf_op jit(solution)/shard_map/pallas_call | solution.py:305
  37.7 1.8 %copy.7 = bf16[1,1,3,256,256]{4,3,2,1,0:T(8,128)(2,1)} copy(bf16[1,1,3,256,256]{4,3,2,1,0:T(8,128)(2,1)} %shard_map.55) | data formatting | bytes 786432

commit v3 on v2

v3 whole, which is shorter than its diff:
```python
import functools

import jax
import jax.numpy as jnp
from jax import lax
from jax.experimental import pallas as pl
from jax.experimental.pallas import tpu as pltpu
from jax.sharding import PartitionSpec as P

MESH = pl.DeviceIdType.MESH
TINY = 1.2e-34
TOP = 32767.0
HOLDS = 0b10110000
BELOW_LATE = 0b11100000
LEFT_LATE = 0b10000000


def split(value):
    high = value.astype(jnp.bfloat16)
    low = (value - high.astype(jnp.float32)).astype(jnp.bfloat16)
    return high, low


def kernel(
    a_hbm, rows, b_hbm, cols, pattern, out,
    a_in, b_in, a_send, b_send, a_got, b_got,
    a_scale, b_scale, a_scale_got, b_scale_got,
    a_high, a_low, b_high, b_low, total,
    load_sem, a_send_sem, b_send_sem, a_recv_sem, b_recv_sem, below_in, left_in, sent,
):
    n_row, n_col = lax.axis_size("row"), lax.axis_size("col")
    r, c = lax.axis_index("row"), lax.axis_index("col")
    panel_rows, width = rows.shape[2], rows.shape[3]
    size = a_in.shape[-1]
    groups = panel_rows * panel_rows
    both, either, no = jnp.logical_and, jnp.logical_or, jnp.logical_not

    core, half, lane = lax.rem(r, 2), lax.rem(lax.div(r, 2), 2), lax.rem(c, 4)
    late = half == 1
    early = no(late)

    def listed(table, half, lane):
        return lax.rem(lax.shift_right_logical(table, half * 4 + lane), 2)

    near, far = core == 1, core == 0
    holds_b = both(late, listed(HOLDS, half, lane) == 1)
    holds_a = both(early, listed(HOLDS, half, lane) == 1)

    c_up, c_left = lax.rem(c + 1, n_col), lax.rem(c + n_col - 1, n_col)
    r_up = lax.rem(r + 1, n_row)
    target = (lax.rem(r + n_row - 1, n_row), c)
    up = (r_up, c)
    right, left = (r, c_up), (r, c_left)

    loads = []
    for k in range(panel_rows):
        part = pl.ds(k * width, width)
        for n, (source, into) in enumerate(((a_hbm, a_in), (b_hbm, b_in))):
            copy = pltpu.make_async_copy(source.at[0, 0, part], into.at[part], load_sem.at[n, k])
            copy.start()
            loads.append(copy)

    barrier = pltpu.get_barrier_semaphore()
    target_later = either(near, early)
    source_later = both(near, early)
    right_later, left_later = lane < 3, lane == 0

    def signal(sem, device):
        pl.semaphore_signal(sem, inc=1, device_id=device, device_id_type=MESH)

    before = 0
    for later, device in (
        (source_later, up), (target_later, target), (right_later, right), (left_later, left),
    ):
        pl.when(later)(functools.partial(signal, barrier, device))
        before = before + jnp.where(later, 0, 1)

    @pl.when(before > 0)
    def _():
        pl.semaphore_wait(barrier, before)

    def answer_below():
        pl.when(no(source_later))(functools.partial(signal, below_in, up))

    def answer_left():
        pl.when(no(right_later))(functools.partial(signal, left_in, right))

    below_waits = both(both(late, near), listed(BELOW_LATE, half, lane) == 1)
    left_waits = both(late, listed(LEFT_LATE, half, lane) == 1)
    pl.when(no(below_waits))(answer_below)
    pl.when(no(left_waits))(answer_left)

    def await_target():
        @pl.when(target_later)
        def _():
            pl.semaphore_wait(below_in, 1)

    def await_left():
        @pl.when(left_later)
        def _():
            pl.semaphore_wait(left_in, 1)

    def send(source, into, send_sem, recv_sem, device):
        return pltpu.make_async_remote_copy(
            src_ref=source, dst_ref=into, send_sem=send_sem, recv_sem=recv_sem,
            device_id=device, device_id_type=MESH,
        )

    def a_copy(at):
        sems = a_send_sem.at[at], a_recv_sem.at[at]
        if at >= groups:
            return send(a_scale.at[at - groups], a_scale_got.at[at - groups], *sems, target)
        return send(a_send.at[at], a_got.at[at], *sems, target)

    def b_copy(at):
        sems = b_send_sem.at[at], b_recv_sem.at[at]
        if at >= groups:
            return send(b_scale.at[at - groups], b_scale_got.at[at - groups], *sems, left)
        return send(b_send.at[at], b_got.at[at], *sems, left)

    def part_of(k):
        return [k * panel_rows + i for i in range(panel_rows)] + [groups + k]

    def each(copy, act, *more):
        for k in range(panel_rows):
            for at in part_of(k):
                getattr(copy(at, *more), act)()

    def coded(value, queue, scale, k, i):
        peak = jnp.maximum(jnp.max(jnp.abs(value), axis=0, keepdims=True), TINY)
        queue[k * panel_rows + i] = jnp.round(value * (TOP / peak)).astype(jnp.int32).astype(jnp.int16)
        scale[k, pl.ds(i, 1), :] = peak * (1.0 / TOP)

    def decoded(queue, scale, k, i):
        return queue[k * panel_rows + i].astype(jnp.int32).astype(jnp.float32) * scale[k, pl.ds(i, 1), :]

    def summed(labels, blocks, k, want):
        value = None
        for m in range(width):
            weight = (labels[0, 0, k, m] == want).astype(jnp.float32)
            term = blocks[k * width + m].astype(jnp.float32) * weight
            value = term if value is None else value + term
        return value

    def prepare_a():
        for k in range(panel_rows):
            span = pl.ds(k * size, size)
            loads[2 * k].wait()
            for i in range(panel_rows):
                value = summed(rows, a_in, k, i)
                coded(value, a_send, a_scale, k, i)
                a_high[i, :, span], a_low[i, :, span] = split(value)
                yield k * panel_rows + i
            yield groups + k

    def prepare_b():
        for k in range(panel_rows):
            span = pl.ds(k * size, size)
            loads[2 * k + 1].wait()
            for j in range(panel_rows):
                value = summed(cols, b_in, k, j)
                coded(value, b_send, b_scale, k, j)
                b_high[j, span, :], b_low[j, span, :] = split(value)
                yield k * panel_rows + j
            yield groups + k

    @pl.when(early)
    def _():
        for at in prepare_b():
            if at == 0:
                await_left()
            b_copy(at).start()
        for at in prepare_a():
            pass

    @pl.when(late)
    def _():
        for at in prepare_a():
            pl.when(far)(a_copy(at).start)
        for at in prepare_b():
            pass

    @pl.when(near)
    def _():
        await_target()
        each(a_copy, "start")

    @pl.when(both(late, no(holds_b)))
    def _():
        await_left()
        each(b_copy, "start")

    def product(i, j, span):
        ah, al, bh, bl = a_high[i, :, span], a_low[i, :, span], b_high[j, span, :], b_low[j, span, :]
        dot = lambda x, y: jnp.dot(x, y, preferred_element_type=jnp.float32)
        return dot(ah, bh) + (dot(ah, bl) + dot(al, bh) + dot(al, bl))

    kept = pattern.shape[2]
    for n in range(kept):
        block = pattern[0, 0, n]
        total[n] = product(block >> 1, block & 1, pl.ds(0, panel_rows * size))

    @pl.when(both(early, far))
    def _():
        await_target()
        pl.when(holds_a)(functools.partial(each, b_copy, "wait_send"))
        each(a_copy, "start")

    pl.when(below_waits)(answer_below)
    pl.when(left_waits)(answer_left)

    @pl.when(holds_b)
    def _():
        @pl.when(far)
        def _():
            each(a_copy, "wait_send")
            signal(sent, up)

        @pl.when(near)
        def _():
            pl.semaphore_wait(sent, 1)

        await_left()
        each(b_copy, "start")

    def take_a(k):
        span = pl.ds(k * size, size)
        for at in part_of(k):
            a_copy(at).wait_recv()
        for i in range(panel_rows):
            a_high[i, :, span], a_low[i, :, span] = split(decoded(a_got, a_scale_got, k, i))

    def take_b(k):
        span = pl.ds(k * size, size)
        for at in part_of(k):
            b_copy(at).wait_recv()
        for j in range(panel_rows):
            b_high[j, span, :], b_low[j, span, :] = split(decoded(b_got, b_scale_got, k, j))

    for k in range(panel_rows):
        @pl.when(early)
        def _():
            take_b(k)
            take_a(k)

        @pl.when(late)
        def _():
            take_a(k)
            take_b(k)

        for n in range(kept):
            block = pattern[0, 0, n]
            value = total[n] + product(block >> 1, block & 1, pl.ds(k * size, size))
            if k < panel_rows - 1:
                total[n] = value
            else:
                out[0, 0, n] = value.astype(out.dtype)

    @pl.when(no(both(far, holds_b)))
    def _():
        each(a_copy, "wait_send")

    @pl.when(no(both(far, holds_a)))
    def _():
        each(b_copy, "wait_send")


def body(a_blocks, a_rows, b_blocks, b_cols, c_pattern):
    slots, size = a_blocks.shape[2], a_blocks.shape[-1]
    panel_rows = a_rows.shape[2]
    kept = c_pattern.shape[2]
    groups = panel_rows * panel_rows
    smem = pl.BlockSpec(memory_space=pltpu.SMEM)
    anywhere = pl.BlockSpec(memory_space=pl.ANY)
    bf16, f32 = jnp.bfloat16, jnp.float32
    depth = panel_rows * size
    queue = pltpu.VMEM((groups, size, size), jnp.int16)
    scale = pltpu.VMEM((panel_rows, 8, size), f32)
    regular = pltpu.SemaphoreType.REGULAR
    sems = pltpu.SemaphoreType.DMA((groups + panel_rows,))
    return pl.pallas_call(
        kernel,
        out_shape=jax.ShapeDtypeStruct((1, 1, kept, size, size), bf16),
        in_specs=[anywhere, smem, anywhere, smem, smem],
        out_specs=pl.BlockSpec(memory_space=pltpu.VMEM),
        scratch_shapes=[
            pltpu.VMEM((slots, size, size), bf16), pltpu.VMEM((slots, size, size), bf16),
            queue, queue, queue, queue, scale, scale, scale, scale,
            pltpu.VMEM((panel_rows, size, depth), bf16), pltpu.VMEM((panel_rows, size, depth), bf16),
            pltpu.VMEM((panel_rows, depth, size), bf16), pltpu.VMEM((panel_rows, depth, size), bf16),
            pltpu.VMEM((kept, size, size), f32),
            pltpu.SemaphoreType.DMA((2, panel_rows)), sems, sems, sems, sems, regular, regular, regular,
        ],
        compiler_params=pltpu.CompilerParams(
            collective_id=0, has_side_effects=True, vmem_limit_bytes=60 << 20
        ),
        cost_estimate=pl.CostEstimate(flops=64 * 2 * size**3, bytes_accessed=3 << 20, transcendentals=0),
    )(a_blocks, a_rows, b_blocks, b_cols, c_pattern)


def solution(mesh):
    in_specs = (
        P("row", "col", None, None, None),
        P("row", "col", None, None),
        P("row", "col", None, None, None),
        P("row", "col", None, None),
        P("row", "col", None),
    )
    out_specs = P("row", "col", None, None, None)
    return jax.shard_map(body, mesh=mesh, in_specs=in_specs, out_specs=out_specs, check_vma=False)
```

time: 39.7 us -> 37.4 us (0.942)
  the two profiles are of different devices: /device:TPU:319 before, /device:TPU:369 now
where the time goes in v3:
time: 37.4 us; the launch traced here: 37.2 us
  Pallas kernels  35.4 us (95%)
  local copies, waits for them, and re-layouts  1.77 us (5%)
    pallas_call x1, Pallas kernels, body(): pl.pallas_call(kernel, out_shape=jax.ShapeDtypeStruct((1, 1, kept, size,...  35.4 us
    unnamed x1, local copies, waits for them, and re-layouts  1.77 us

profile of v3, /device:TPU:369, one launch (start us, length us, event | category | flops | bytes accessed | tf_op | source)
XLA Modules:
  0.0 37.2 jit_solution(6720810558614265165)
XLA Ops:
  0.0 35.4 %shard_map.55 = bf16[1,1,3,256,256]{4,3,2,1,0:T(8,128)(2,1)} custom-call(bf16[1,1,8,256,256]{4,3,2,1,0:T(8,128)(2,1)} %a_hbm.1, s32[1,1,2,4]{3,2,1,0:T(2,128)} %rows.1, bf16[1,1,8,256,256]{4,3,2,1,0:T(8,128)(2,1)} %b_hbm.1, s32[1,1,2,4]{3,2,1,0:T(2,128)} %cols.1, s32[1,1,3]{2,1,0:T(1,128)} %pattern.1), custom_call_target="tpu_custom_call" | custom-call | flops 2147483648 | bytes 3145728 | tf_op jit(solution)/shard_map/pallas_call | solution.py:281
  35.4 1.8 %copy.7 = bf16[1,1,3,256,256]{4,3,2,1,0:T(8,128)(2,1)} copy(bf16[1,1,3,256,256]{4,3,2,1,0:T(8,128)(2,1)} %shard_map.55) | data formatting | bytes 786432

commit v4 on v3

--- a/solution.py
+++ b/solution.py
@@ -56,9 +56,9 @@
     for k in range(panel_rows):
         part = pl.ds(k * width, width)
         for n, (source, into) in enumerate(((a_hbm, a_in), (b_hbm, b_in))):
-            copy = pltpu.make_async_copy(source.at[0, 0, part], into.at[part], load_sem.at[n, k])
-            copy.start()
-            loads.append(copy)
+            loads.append(pltpu.make_async_copy(source.at[0, 0, part], into.at[part], load_sem.at[n, k]))
+    for copy in loads[0::2] + loads[1::2]:
+        copy.start()
 
     barrier = pltpu.get_barrier_semaphore()
     target_later = either(near, early)

time: 37.4 us -> 37.4 us (level)
  no operation moved by 1% of the time
where the time goes in v4:
time: 37.4 us; the launch traced here: 37.2 us
  Pallas kernels  35.4 us (95%)
  local copies, waits for them, and re-layouts  1.77 us (5%)
    pallas_call x1, Pallas kernels, body(): pl.pallas_call(kernel, out_shape=jax.ShapeDtypeStruct((1, 1, kept, size,...  35.4 us
    unnamed x1, local copies, waits for them, and re-layouts  1.77 us

profile of v4, /device:TPU:369, one launch (start us, length us, event | category | flops | bytes accessed | tf_op | source)
XLA Modules:
  0.0 37.2 jit_solution(11994366333234501618)
XLA Ops:
  0.0 35.4 %shard_map.55 = bf16[1,1,3,256,256]{4,3,2,1,0:T(8,128)(2,1)} custom-call(bf16[1,1,8,256,256]{4,3,2,1,0:T(8,128)(2,1)} %a_hbm.1, s32[1,1,2,4]{3,2,1,0:T(2,128)} %rows.1, bf16[1,1,8,256,256]{4,3,2,1,0:T(8,128)(2,1)} %b_hbm.1, s32[1,1,2,4]{3,2,1,0:T(2,128)} %cols.1, s32[1,1,3]{2,1,0:T(1,128)} %pattern.1), custom_call_target="tpu_custom_call" | custom-call | flops 2147483648 | bytes 3145728 | tf_op jit(solution)/shard_map/pallas_call | solution.py:281
  35.4 1.8 %copy.7 = bf16[1,1,3,256,256]{4,3,2,1,0:T(8,128)(2,1)} copy(bf16[1,1,3,256,256]{4,3,2,1,0:T(8,128)(2,1)} %shard_map.55) | data formatting | bytes 786432
